TPU v7x, 32 devices: a whole 2x2x4 slice. The times are simulated.
32 devices in a mesh: mgroup: 8 (over z, core), msub: 4 (over y, x).
Axes of the slice: x: 2, y: 2, z: 4, core: 2. Of those that a mesh axis runs over, the one named last changes fastest.
Arguments:
- in_modes: int32 [32, 2], P(('mgroup', 'msub')), may hold values from 0 to 31
- back_first: bfloat16 [32, 1024, 2048], P(('mgroup', 'msub')), may hold values from -48 to 48
- back_second: bfloat16 [32, 1024, 2048], P(('mgroup', 'msub')), may hold values from -144 to 144
Outputs:
- mask_first: float32 [1024, 2048], P(('mgroup', 'msub'))
- mask_second: float32 [1024, 2048], P(('mgroup', 'msub'))
Inputs may be any that keep to these rules, and one draw needn't show every extreme that they name: `in_modes`: each row holds a mode's row order and column order.
All inputs are finite; a program needn't handle non-finite values.
Results may differ from a plain program's by a relative error of at most 0.013.
Values may be sent and summed in bfloat16 or wider, within the bound.
A program may use at most 128 MiB of HBM per device.

v0:
```python
import math

import jax
import jax.numpy as jnp
from jax import lax
from jax.sharding import PartitionSpec as P

ORDERS = 32


span_width = 24.0


def grid_points(cells):
    index = jnp.arange(cells, dtype=jnp.float32)
    return (index - cells / 2 + 0.5) * (span_width / cells)


def hermite_table(points):
    before = jnp.zeros_like(points)
    current = math.pi ** (-0.25) * jnp.exp(-0.5 * points * points)
    collected = []
    for order in range(ORDERS):
        collected.append(current)
        following = (
            math.sqrt(2.0 / (order + 1)) * points * current
            - math.sqrt(order / (order + 1.0)) * before
        )
        before, current = (current, following)
    return jnp.stack(collected, axis=0)


def chirp_parts(cells):
    index = jnp.arange(cells, dtype=jnp.int32)
    offset = index[:, None] - index[None, :]
    square = offset * offset % (2 * cells)
    phase = square.astype(jnp.float32) * (math.pi / cells)
    factor = cells ** (-0.5)
    return (
        (jnp.cos(phase) * factor).astype(jnp.bfloat16),
        (jnp.sin(phase) * factor).astype(jnp.bfloat16),
    )


def soften(intersection):
    half = intersection.shape[-1] // 2
    real_part = intersection[..., :half]
    imag_part = intersection[..., half:]
    denom = jnp.sqrt(real_part * real_part + imag_part * imag_part + 1.0)
    return intersection / jnp.concatenate([denom, denom], axis=-1)


def pick_funcs(orders, herm_table):
    one_hot = (orders[:, None] == jnp.arange(herm_table.shape[0], dtype=jnp.int32)[None, :]).astype(
        jnp.float32
    )
    return jnp.dot(one_hot, herm_table, precision=lax.Precision.HIGHEST)


def intersection_first(back_rows, field_rows):
    widened = field_rows.astype(jnp.float32)
    tiled = jnp.concatenate([widened, widened], axis=2)
    return jnp.sum(back_rows.astype(jnp.float32) * tiled, axis=0)


def propagate_rows(mask_rows, field_rows, big_chirp):
    widened = field_rows.astype(jnp.float32)
    tiled = jnp.concatenate([widened, widened], axis=2)
    applied = (mask_rows.astype(jnp.float32)[None] * tiled).astype(jnp.bfloat16)
    return jnp.einsum("mrk,kc->mrc", applied, big_chirp, preferred_element_type=jnp.float32).astype(
        jnp.bfloat16
    )


def intersection_conj(back_rows, arrived, cells):
    back_real = back_rows[:, :, :cells]
    back_imag = back_rows[:, :, cells:]
    arr_real = arrived[:, :, :cells]
    arr_imag = arrived[:, :, cells:]
    real_part = jnp.sum(back_real * arr_real + back_imag * arr_imag, axis=0)
    imag_part = jnp.sum(back_imag * arr_real - back_real * arr_imag, axis=0)
    return jnp.concatenate([real_part, imag_part], axis=1)


def body(in_modes, back_first, back_second):
    mode_dev = in_modes.shape[0]
    cells = back_first.shape[1]
    groups_sub = lax.axis_size("msub")
    devices_all = lax.axis_size("mgroup") * groups_sub
    strip_rows = cells // devices_all
    scale_all = float(mode_dev * devices_all) ** (-0.5)
    herm_table = hermite_table(grid_points(cells))
    row_funcs = pick_funcs(in_modes[:, 0], herm_table)
    col_funcs = pick_funcs(in_modes[:, 1], herm_table)
    fields = (row_funcs[:, :, None] * col_funcs[:, None, :]).astype(jnp.bfloat16)
    chirp_real, chirp_imag = chirp_parts(cells)
    big_chirp = jnp.concatenate(
        [
            jnp.concatenate([chirp_real, chirp_imag], axis=1),
            jnp.concatenate([-chirp_imag, chirp_real], axis=1),
        ],
        axis=0,
    )
    back_rows = back_first
    summed = lax.psum(intersection_first(back_rows, fields), ("mgroup", "msub"))
    full_mask = soften(summed * scale_all)
    own_start = lax.axis_index(("mgroup", "msub")) * strip_rows
    mask_first = lax.dynamic_slice_in_dim(full_mask, own_start, strip_rows, 0)
    spread = propagate_rows(full_mask.astype(jnp.bfloat16), fields, big_chirp)
    rotated = jnp.concatenate([-spread[:, :, cells:], spread[:, :, :cells]], axis=2)
    arrived = jnp.einsum("rk,mkc->mrc", chirp_real, spread, preferred_element_type=jnp.float32)
    arrived = arrived + jnp.einsum(
        "rk,mkc->mrc", chirp_imag, rotated, preferred_element_type=jnp.float32
    )
    back_rows = back_second.astype(jnp.float32)
    outer_block = lax.psum_scatter(
        intersection_conj(back_rows, arrived, cells), "mgroup", scatter_dimension=0, tiled=True
    )
    summed_two = lax.psum_scatter(outer_block, "msub", scatter_dimension=0, tiled=True)
    mask_second = soften(summed_two * scale_all)
    return (mask_first, mask_second)


def solution(mesh):
    placed = (
        P(("mgroup", "msub"), None),
        P(("mgroup", "msub"), None, None),
        P(("mgroup", "msub"), None, None),
    )
    return jax.shard_map(
        body,
        mesh=mesh,
        in_specs=placed,
        out_specs=(P(("mgroup", "msub"), None), P(("mgroup", "msub"), None)),
        check_vma=False,
    )
```

profile of v0, /device:TPU:0, one launch (start us, length us, event | category | flops | bytes accessed | tf_op | source)
XLA Modules:
  0.0 408.0 jit_solution(17125098738103923876)
XLA Ops:
  7.2 0.0 all-reduce.2.cloned.1.call-start
  7.3 0.1 multiply_subtract_fusion.24
  7.4 0.1 multiply_subtract_fusion.22
  7.5 0.1 multiply_subtract_fusion.20
  7.5 0.1 multiply_subtract_fusion.18
  7.6 0.1 multiply_subtract_fusion.16
  7.7 0.1 multiply_subtract_fusion.14
  7.9 0.1 multiply_subtract_fusion.12
  8.0 0.1 multiply_subtract_fusion.10
  8.1 0.1 multiply_subtract_fusion.8
  8.3 0.2 multiply_subtract_fusion.6
  8.4 0.2 multiply_subtract_fusion.4
  8.6 0.2 multiply_subtract_fusion.2
  8.8 0.2 multiply_subtract_fusion
  9.0 1.3 fusion.51
  10.3 0.2 stack.2
  10.5 0.8 fusion.29
  11.3 0.8 fusion.31
  12.1 0.3 multiply_convert_fusion.5
  12.4 5.6 %multiply_bitcast_fusion = f32[1024,2048]{1,0:T(8,128)} fusion(bf16[1,1024,2048]{2,1,0:T(8,128)(2,1)} %param.4, bf16[1,1024,1024]{2,1,0:T(8,128)(2,1)S(1)} %multiply_convert_fusion.5), kind=kLoop, calls=%fused_computation.12 | loop fusion | flops 12582912 | bytes 14680064 | tf_op jit(solution)/shard_map/reduce_sum | solution.py:63
  18.1 0.0 all-reduce.2.cloned.1.call-update
  18.1 0.0 reduce-scatter.5.cloned.1.call-start
  18.2 6.3 %copy.12 = bf16[1,1024,2048]{1,2,0:T(8,128)(2,1)} copy(bf16[1,1024,2048]{2,1,0:T(8,128)(2,1)} %param.5) | data formatting | bytes 8388608 | tf_op args[2]
  24.5 6.8 %convert_element_type.80 = f32[1,1024,2048]{1,2,0:T(8,128)} convert(bf16[1,1024,2048]{1,2,0:T(8,128)(2,1)} %copy.12) | non-fusion elementwise | flops 2097152 | bytes 12582912 | tf_op jit(solution)/shard_map/convert_element_type | solution.py:115
  31.2 0.3 multiply_convert_fusion.4
  31.5 16.7 %fusion.24 = bf16[1024,1024]{1,0:T(8,128)(2,1)} fusion(), kind=kLoop, calls=%fused_computation.41 | loop fusion | flops 20971520 | bytes 2097152 | tf_op jit(solution)/shard_map/neg | solution.py:100
  48.3 18.1 %multiply_convert_fusion.2 = (bf16[1024,1024]{1,0:T(8,128)(2,1)}, bf16[1024,1024]{1,0:T(8,128)(2,1)}) fusion(), kind=kLoop, calls=%fused_computation.33 | loop fusion | flops 19922944 | bytes 4194304 | tf_op jit(solution)/shard_map/convert_element_type | solution.py:41
  66.4 133.2 %all-reduce.2.cloned.1.call-done = f32[1024,2048]{1,0:T(8,128)} async-done(((f32[1024,2048]{1,0:T(8,128)}), f32[1024,2048]{1,0:T(8,128)}) %all-reduce.2.cloned.1.call-update) | async-done | bytes 8388624 | tf_op jit(solution)/shard_map/psum | solution.py:105
  199.6 5.2 %broadcast_multiply_fusion = f32[1024,2048]{1,0:T(8,128)S(1)} fusion(f32[1024,2048]{1,0:T(8,128)} %all-reduce.2.cloned.1.call-done), kind=kLoop, calls=%fused_computation.37 | loop fusion | flops 2097152 | bytes 16777216 | tf_op jit(solution)/shard_map/mul | solution.py:106
  204.8 0.0 copy-start
  204.8 1.6 fusion.13
  206.4 1.8 copy-done
  208.2 4.8 %maximum_divide_fusion = f32[1024,2048]{1,0:T(8,128)} fusion(f32[1024,1024]{1,0:T(8,128)S(1)} %fusion.13, f32[1024,2048]{1,0:T(8,128)S(1)} %copy-done), kind=kLoop, calls=%fused_computation | loop fusion | flops 6291456 | bytes 20971520 | tf_op jit(solution)/shard_map/div | solution.py:50
  213.0 16.5 %fusion.21 = bf16[1024,2048]{1,0:T(8,128)(2,1)} fusion(bf16[1024,1024]{1,0:T(8,128)(2,1)} %get-tuple-element.47, bf16[1024,1024]{1,0:T(8,128)(2,1)} %fusion.24, bf16[1024,1024]{1,0:T(8,128)(2,1)} %get-tuple-element.46, bf16[1024,1024]{1,0:T(8,128)(2,1)S(1)} %multiply_convert_fusion.4, f32[1024,2048]{1,0:T(8,128)} %maximum_divide_fusion), kind=kOutput, calls=%fused_computation.39 | convolution fusion | flops 8642363392 | bytes 20971520 | tf_op jit(solution)/shard_map/mrk,kc->mrc/dot_general | solution.py:70
  229.5 0.0 slice-start
  229.5 2.6 slice_negate_fusion
  232.2 0.0 copy-start.1
  232.2 0.0 slice-start.1
  232.2 19.0 %fusion.17 = f32[2048,1024]{1,0:T(8,128)S(1)} fusion(bf16[1,1024,1024]{2,1,0:T(8,128)(2,1)S(1)} %get-tuple-element.11, bf16[1,1024,1024]{2,1,0:T(8,128)(2,1)S(1)} %get-tuple-element.10), kind=kOutput, calls=%fused_computation.28 | convolution fusion | flops 4321181696 | bytes 12582912 | tf_op jit(solution)/shard_map/rk,mkc->mrc/dot_general | solution.py:112
  251.2 0.0 copy-done.1
  251.2 22.1 %add_bitcast_fusion = f32[1,1024,2048]{1,2,0:T(8,128)S(1)} fusion(f32[2048,1024]{1,0:T(8,128)S(1)} %fusion.17, bf16[1024,2048]{1,0:T(8,128)(2,1)S(1)} %copy-done.1), kind=kOutput, calls=%fused_computation.10 | convolution fusion | flops 4314890240 | bytes 20971520 | tf_op jit(solution)/shard_map/rk,mkc->mrc/dot_general | solution.py:111
  273.3 0.0 slice-done
  273.3 0.0 slice-done.1
  273.3 2.0 add_bitcast_fusion.1
  275.3 4.1 pad_maximum_fusion
  279.4 0.0 reduce-scatter.5.cloned.1.call-update
  279.4 0.0 reduce-scatter.7.cloned.1.call-start
  279.5 89.8 %reduce-scatter.5.cloned.1.call-done = f32[128,2048]{0,1:T(8,128)} async-done(((f32[1024,2048]{0,1:T(8,128)}), f32[128,2048]{0,1:T(8,128)}) %reduce-scatter.5.cloned.1.call-update) | async-done | bytes 1048592 | tf_op jit(solution)/shard_map/reduce_scatter | solution.py:116
  369.2 2.6 copy.14
  371.9 0.0 reduce-scatter.7.cloned.1.call-update
  371.9 1.7 constant_dynamic-slice_fusion
  373.6 24.7 %reduce-scatter.7.cloned.1.call-done = f32[32,2048]{1,0:T(8,128)} async-done(((f32[128,2048]{1,0:T(8,128)}), f32[32,2048]{1,0:T(8,128)}) %reduce-scatter.7.cloned.1.call-update) | async-done | bytes 262160
  398.2 1.3 copy.15
  399.5 0.1 broadcast_multiply_fusion.1
  399.6 0.2 fusion.27
  399.8 0.1 maximum_divide_fusion.1
  400.0 1.0 copy.13
  (4 shorter events, 0.1 us)
Async XLA Ops:
  7.2 192.5 %all-reduce.2.cloned.1.call-start = ((), (), s32[]{:S(2)}) async-start(), calls=%async_computation.2 | async-start | bytes 16777216 | tf_op jit(solution)/shard_map/psum | solution.py:105
  18.1 351.1 %reduce-scatter.5.cloned.1.call-start = ((), (), s32[]{:S(2)}) async-start(), calls=%async_computation.3 | async-start | bytes 9437184 | tf_op jit(solution)/shard_map/reduce_scatter | solution.py:116
  204.8 3.4 copy-start
  229.5 43.8 %slice-start = ((s8[8388608]{0:T(1024)(128)(4,1)}), s8[4194304]{0:T(1024)(128)(4,1)S(1)}, s32[]{:S(2)}) async-start(s8[8388608]{0:T(1024)(128)(4,1)} %bitcast.28), calls=%async_computation.5 | async-start | bytes 8388608
  232.2 19.0 %copy-start.1 = (bf16[1024,2048]{1,0:T(8,128)(2,1)S(1)}, bf16[1024,2048]{1,0:T(8,128)(2,1)}, u32[]{:S(2)}) copy-start(bf16[1024,2048]{1,0:T(8,128)(2,1)} %fusion.21) | copy-start | bytes 12582916
  232.2 41.1 %slice-start.1 = ((s8[8388608]{0:T(1024)(128)(4,1)}), s8[4194304]{0:T(1024)(128)(4,1)S(1)}, s32[]{:S(2)}) async-start(s8[8388608]{0:T(1024)(128)(4,1)} %bitcast.28), calls=%async_computation.6 | async-start | bytes 8388608
  279.4 118.8 %reduce-scatter.7.cloned.1.call-start = ((), (), s32[]{:S(2)}) async-start(), calls=%async_computation.4 | async-start | bytes 1310720
Sparse Core Ops, SparseCore 0:
  18.2 181.3 all-reduce.1
  279.5 89.6 reduce-scatter.4
  372.1 26.0 reduce-scatter.6
where the time goes:
time: 416 us; the launch traced here: 408 us
  waiting for transfers between devices  248 us (60%)
  other arithmetic  70.3 us (17%)
  matrix products  59.2 us (14%)
  local copies, waits for them, and re-layouts  16.3 us (4%)
  between operations  14.4 us (3%)
    psum x1, waiting for transfers between devices, body(): summed = lax.psum(intersection_first(back_rows, fields), ('mgroup', 'msub'))  133 us
    reduce_scatter x1, waiting for transfers between devices, body(): lax.psum_scatter(intersection_conj(back_rows, arrived, cells), 'mgroup',...  89.8 us
    unnamed x4, waiting for transfers between devices  24.7 us
    dot_general x1, matrix products, body(): jnp.einsum('rk,mkc->mrc', chirp_real, spread, preferred_element_type=jnp....  22.1 us
    dot_general x1, matrix products, body(): jnp.einsum('rk,mkc->mrc', chirp_imag, rotated, preferred_element_type=jnp...  19 us
    convert_element_type x1, other arithmetic, chirp_parts(): (jnp.sin(phase) * factor).astype(jnp.bfloat16)  18.1 us
    neg x1, other arithmetic, body(): -chirp_imag  16.7 us
    dot_general x1, matrix products, propagate_rows(): jnp.einsum('mrk,kc->mrc', applied, big_chirp, preferred_element_type=jnp....  16.5 us
  transfers between devices with their start and end apart: 3, of which 3 were waited for; matrix products, arithmetic and copies ran while one was open for 12% of the time, Pallas kernels for 0%

commit v1 on v0

v1 whole, which is shorter than its diff:
```python
import functools
import math

import jax
import jax.numpy as jnp
from jax import lax
from jax.experimental import pallas as pl
from jax.experimental.pallas import tpu as pltpu
from jax.sharding import PartitionSpec as P

ORDERS = 32


span_width = 24.0


def grid_points(cells):
    index = jnp.arange(cells, dtype=jnp.float32)
    return (index - cells / 2 + 0.5) * (span_width / cells)


def hermite_table(points):
    before = jnp.zeros_like(points)
    current = math.pi ** (-0.25) * jnp.exp(-0.5 * points * points)
    collected = []
    for order in range(ORDERS):
        collected.append(current)
        following = (
            math.sqrt(2.0 / (order + 1)) * points * current
            - math.sqrt(order / (order + 1.0)) * before
        )
        before, current = (current, following)
    return jnp.stack(collected, axis=0)


def chirp_parts(cells):
    index = jnp.arange(cells, dtype=jnp.int32)
    offset = index[:, None] - index[None, :]
    square = offset * offset % (2 * cells)
    phase = square.astype(jnp.float32) * (math.pi / cells)
    factor = cells ** (-0.5)
    return (
        (jnp.cos(phase) * factor).astype(jnp.bfloat16),
        (jnp.sin(phase) * factor).astype(jnp.bfloat16),
    )


def soften(intersection):
    half = intersection.shape[-1] // 2
    real_part = intersection[..., :half]
    imag_part = intersection[..., half:]
    denom = jnp.sqrt(real_part * real_part + imag_part * imag_part + 1.0)
    return intersection / jnp.concatenate([denom, denom], axis=-1)


def pick_funcs(orders, herm_table):
    one_hot = (orders[:, None] == jnp.arange(herm_table.shape[0], dtype=jnp.int32)[None, :]).astype(
        jnp.float32
    )
    return jnp.dot(one_hot, herm_table, precision=lax.Precision.HIGHEST)


def intersection_first(back_rows, field_rows):
    widened = field_rows.astype(jnp.float32)
    tiled = jnp.concatenate([widened, widened], axis=2)
    return jnp.sum(back_rows.astype(jnp.float32) * tiled, axis=0)


def residue_chirp(cells):
    block = cells // 4
    chirp_real, chirp_imag = chirp_parts(cells)
    index = jnp.arange(block, dtype=jnp.int32)
    residue = (index[None, :] - index[:, None]) % 4
    keep = residue[None] == jnp.arange(4, dtype=jnp.int32)[:, None, None]
    real = jnp.where(keep, chirp_real[None, :block, :block], 0)
    imag = jnp.where(keep, chirp_imag[None, :block, :block], 0)
    return jnp.concatenate(
        [jnp.concatenate([real, imag], axis=2), jnp.concatenate([-imag, real], axis=2)], axis=1
    )


def four_sums(real, imag, sign):
    even_r, even_i = real[0] + real[2], imag[0] + imag[2]
    odd_r, odd_i = real[1] + real[3], imag[1] + imag[3]
    low_r, low_i = real[0] - real[2], imag[0] - imag[2]
    top_r, top_i = sign * (real[1] - real[3]), sign * (imag[1] - imag[3])
    return (
        (even_r + odd_r, even_i + odd_i),
        (low_r - top_i, low_i + top_r),
        (even_r - odd_r, even_i - odd_i),
        (low_r + top_i, low_i - top_r),
    )


def split_four(array, axis):
    return jnp.split(array, 4, axis=axis)


def propagate_columns(real, imag, table):
    block = real.shape[1] // 4
    parts = four_sums(split_four(real, 1), split_four(imag, 1), -1.0)
    outs = []
    for r in range(4):
        both = jnp.concatenate(parts[r], axis=1).astype(jnp.bfloat16)
        outs.append(jnp.dot(both, table[r], preferred_element_type=jnp.float32))
    sums = four_sums([o[:, :block] for o in outs], [o[:, block:] for o in outs], 1.0)
    return [jnp.concatenate([s[k] for s in sums], axis=1).astype(jnp.bfloat16) for k in (0, 1)]


def propagate_down(real, imag, table):
    block = real.shape[0] // 4
    parts = four_sums(
        split_four(real.astype(jnp.float32), 0), split_four(imag.astype(jnp.float32), 0), -1.0
    )
    outs = []
    for r in range(4):
        both = jnp.concatenate(parts[r], axis=0).astype(jnp.bfloat16)
        outs.append(jnp.dot(table[r].T, both, preferred_element_type=jnp.float32))
    sums = four_sums([o[:block] for o in outs], [o[block:] for o in outs], 1.0)
    return [jnp.concatenate([s[k] for s in sums], axis=0) for k in (0, 1)]


MESH = pl.DeviceIdType.MESH
CHUNKS = 4
OFFSETS = (0, 1, 3, 4, 5, 6, 7, 8, 9)
OFFSETS_TWO = (0, 1, 2, 3, 4)


def sweep_kernel(
    depth, scale,
    row_ref, col_ref, chirp_ref, first_hbm, second_hbm, out_one, out_two,
    first, second, sums, from_core, from_near, from_far, from_z,
    sums2, from_core2, from_near2, from_far2, from_z2,
    mask, spread, table_col, table_row, local_sem, send_sem, recv_sem,
):
    cells = first.shape[0]
    chunks, strip, width = sums.shape[0], sums.shape[6], sums.shape[7]
    block = cells // depth
    quarter = cells // 4
    group, sub = lax.axis_index("mgroup"), lax.axis_index("msub")
    z, c = group // 2, group % 2
    y, x = sub // 2, sub % 2
    sibling = (z * 2 + 1 - c, sub)
    across_x = (group, y * 2 + 1 - x)
    across_y = (group, (1 - y) * 2 + x)
    along_z = [(lax.rem(z + i, depth) * 2 + c, sub) for i in range(1, depth)]
    near, far = (x, y), (y, x)
    near_dev, far_dev = (across_x, across_y), (across_y, across_x)

    barrier = pltpu.get_barrier_semaphore()
    for peer in [sibling, across_x, across_y] + along_z:
        pl.semaphore_signal(barrier, inc=1, device_id=peer, device_id_type=MESH)

    loads = {}
    def load(name, src, dst):
        copy = pltpu.make_async_copy(src, dst, local_sem.at[len(loads)])
        copy.start()
        loads[name] = copy
    for k in range(chunks):
        for h in range(2):
            at = pl.ds(h * cells + k * width, width)
            load(("first", k, h), first_hbm.at[:, at], first.at[:, at])
    load("second", second_hbm, second)

    pl.semaphore_wait(barrier, 2 + depth)

    sent = []
    def send(src, dst, peer):
        at = len(sent)
        copy = pltpu.make_async_remote_copy(
            src_ref=src, dst_ref=dst, send_sem=send_sem.at[at], recv_sem=recv_sem.at[at],
            device_id=peer, device_id_type=MESH,
        )
        copy.start()
        sent.append(copy)
        return copy

    def field_at(start, rows, k):
        col = col_ref[:, k * width : (k + 1) * width]
        return (row_ref[pl.ds(start, rows), :] * col).astype(jnp.bfloat16).astype(jnp.float32)

    def soften_pair(real, imag):
        factor = lax.rsqrt(real * real + imag * imag + 1.0)
        return real * factor, imag * factor

    wide = lambda value: value.astype(jnp.float32)
    low = lambda value: value.astype(jnp.bfloat16)
    arrivals = {}

    def reduce_stages(tag, acc, rc, rn, rf, rz):
        def core_send(k):
            for h in range(2):
                arrivals[tag, 0, k, h] = send(acc.at[k, h, 1 - c], rc.at[k, h], sibling)

        def near_send(k):
            for h in range(2):
                arrivals[tag, 0, k, h].wait_recv()
                a = 1 - near[h]
                acc[k, h, c, a] = low(wide(acc[k, h, c, a]) + wide(rc[k, h, a]))
                arrivals[tag, 1, k, h] = send(acc.at[k, h, c, a], rn.at[k, h], near_dev[h])

        def far_send(k):
            for h in range(2):
                arrivals[tag, 1, k, h].wait_recv()
                a, b = near[h], 1 - far[h]
                acc[k, h, c, a, b] = low(
                    wide(acc[k, h, c, a, b]) + wide(rc[k, h, a, b]) + wide(rn[k, h, b])
                )
                arrivals[tag, 2, k, h] = send(acc.at[k, h, c, a, b], rf.at[k, h], far_dev[h])

        def z_send(k):
            for h in range(2):
                arrivals[tag, 2, k, h].wait_recv()
                a, b = near[h], far[h]
                for i in range(1, depth):
                    to = lax.rem(z + i, depth)
                    acc[k, h, c, a, b, to] = low(
                        wide(acc[k, h, c, a, b, to]) + wide(rc[k, h, a, b, to])
                        + wide(rn[k, h, b, to]) + wide(rf[k, h, to])
                    )
                    arrivals[tag, 3, k, h, i] = send(
                        acc.at[k, h, c, a, b, to], rz.at[k, h, i - 1], along_z[i - 1]
                    )

        def finish(k):
            totals = []
            for h in range(2):
                a, b = near[h], far[h]
                total = wide(acc[k, h, c, a, b, z]) + wide(rc[k, h, a, b, z])
                total += wide(rn[k, h, b, z]) + wide(rf[k, h, z])
                for i in range(1, depth):
                    arrivals[tag, 3, k, h, i].wait_recv()
                    total += wide(rz[k, h, i - 1])
                totals.append(total * scale)
            return soften_pair(*totals)

        return core_send, near_send, far_send, z_send, finish

    core_send, near_send, far_send, z_send, finish = reduce_stages(
        1, sums, from_core, from_near, from_far, from_z
    )

    def product(k):
        for h in range(2):
            loads["first", k, h].wait()
        def half(part):
            @pl.loop(0, depth)
            def _(zz):
                for yy in range(2):
                    for xx in range(2):
                        start = pl.multiple_of((((zz * 2 + part) * 2 + yy) * 2 + xx) * strip, strip)
                        field = field_at(start, strip, k)
                        for h in range(2):
                            at = h * cells + k * width
                            value = wide(first[pl.ds(start, strip), at : at + width]) * field
                            a, b = ((xx, yy), (yy, xx))[h]
                            sums[k, h, part, a, b, zz] = low(value)
        half(1 - c)
        core_send(k)
        half(c)

    def first_mask(k):
        real, imag = finish(k)
        for h, value in enumerate((real, imag)):
            at = h * cells + k * width
            out_one[:, at : at + width] = value
            a, b = near[h], far[h]
            mask[k, h, c, a, b, z] = low(value)
            for i in range(1, depth):
                arrivals["g", 0, k, h, i] = send(
                    mask.at[k, h, c, a, b, z], mask.at[k, h, c, a, b, z], along_z[i - 1]
                )

    def gather_far(k):
        for h in range(2):
            for i in range(1, depth):
                arrivals["g", 0, k, h, i].wait_recv()
            at = mask.at[k, h, c, near[h], far[h]]
            arrivals["g", 1, k, h] = send(at, at, far_dev[h])

    def gather_near(k):
        for h in range(2):
            arrivals["g", 1, k, h].wait_recv()
            at = mask.at[k, h, c, near[h]]
            arrivals["g", 2, k, h] = send(at, at, near_dev[h])

    def gather_core(k):
        for h in range(2):
            arrivals["g", 2, k, h].wait_recv()
            at = mask.at[k, h, c]
            arrivals["g", 3, k, h] = send(at, at, sibling)

    def gather_done(k):
        for h in range(2):
            arrivals["g", 3, k, h].wait_recv()

    def schedule(stages, offsets, between=None):
        order = sorted(
            (offsets[s] + k, -s, k) for s in range(len(stages)) for k in range(chunks)
        )
        for n, (_, s, k) in enumerate(order):
            if between and n == 2 * chunks:
                between()
            stages[-s](k)

    def build_tables():
        one = lax.broadcasted_iota(jnp.int32, (quarter, quarter), 0)
        two = lax.broadcasted_iota(jnp.int32, (quarter, quarter), 1)
        real, imag = wide(chirp_ref[0]), wide(chirp_ref[1])
        for table, diff, sign in ((table_col, two - one, 1.0), (table_row, one - two, -1.0)):
            for r in range(4):
                keep = (diff & 3) == r
                rr = jnp.where(keep, real, 0.0)
                ii = jnp.where(keep, imag, 0.0)
                table[r, :quarter, :quarter] = low(rr)
                table[r, quarter:, quarter:] = low(rr)
                table[r, :quarter, quarter:] = low(sign * ii)
                table[r, quarter:, :quarter] = low(-sign * ii)

    schedule(
        (product, near_send, far_send, z_send, first_mask, gather_far, gather_near, gather_core, gather_done),
        OFFSETS, build_tables,
    )

    @pl.loop(0, depth)
    def _(zz):
        start = pl.multiple_of(zz * block, block)
        sides = [[], []]
        for q in range(4):
            field = field_at(start, block, q)
            for h in range(2):
                strips = []
                for cc in range(2):
                    for yy in range(2):
                        for xx in range(2):
                            a, b = ((xx, yy), (yy, xx))[h]
                            strips.append(wide(mask[q, h, cc, a, b, zz]))
                value = jnp.concatenate(strips, axis=0) * field
                sides[h].append(wide(low(value)))
        outs = []
        for r, pair in enumerate(four_sums(sides[0], sides[1], -1.0)):
            both = low(jnp.concatenate(pair, axis=1))
            outs.append(jnp.dot(both, table_col[r], preferred_element_type=jnp.float32))
        done = four_sums([o[:, :quarter] for o in outs], [o[:, quarter:] for o in outs], 1.0)
        for p in range(4):
            for h in range(2):
                spread[p, h, pl.ds(start, block), :] = low(done[p][h])

    core_send2, near_send2, far_send2, z_send2, finish2 = reduce_stages(
        2, sums2, from_core2, from_near2, from_far2, from_z2
    )

    def arrive(k):
        if k == 0:
            loads["second"].wait()
        sides = [
            [wide(spread[k, h, q * quarter : (q + 1) * quarter, :]) for q in range(4)] for h in range(2)
        ]
        outs = []
        for r, pair in enumerate(four_sums(sides[0], sides[1], -1.0)):
            both = low(jnp.concatenate(pair, axis=0))
            outs.append(jnp.dot(table_row[r], both, preferred_element_type=jnp.float32))
        done = four_sums([o[:quarter] for o in outs], [o[quarter:] for o in outs], 1.0)
        for p in range(4):
            rows = slice(p * quarter, (p + 1) * quarter)
            back_real = wide(second[rows, k * width : (k + 1) * width])
            back_imag = wide(second[rows, cells + k * width : cells + (k + 1) * width])
            arr_real, arr_imag = done[p]
            terms = (
                back_real * arr_real + back_imag * arr_imag,
                back_imag * arr_real - back_real * arr_imag,
            )
            for h in range(2):
                value = low(terms[h])
                for n in range(quarter // strip):
                    number = p * (quarter // strip) + n
                    xx, yy, cc, zz = number % 2, number // 2 % 2, number // 4 % 2, number // 8
                    a, b = ((xx, yy), (yy, xx))[h]
                    sums2[k, h, cc, a, b, zz] = value[n * strip : (n + 1) * strip]
        core_send2(k)

    def second_mask(k):
        real, imag = finish2(k)
        out_two[:, k * width : (k + 1) * width] = real
        out_two[:, cells + k * width : cells + (k + 1) * width] = imag

    schedule((arrive, near_send2, far_send2, z_send2, second_mask), OFFSETS_TWO)
    for copy in sent:
        copy.wait_send()


def sweep_call(row_func, col_func, chirp, back_first, back_second, devices, depth, scale):
    cells = back_first.shape[0]
    strip, width, chunks = cells // devices, cells // CHUNKS, CHUNKS
    low = jnp.bfloat16
    tail = (strip, width)
    received = [
        pltpu.VMEM((chunks, 2, 2, 2, depth) + tail, low),
        pltpu.VMEM((chunks, 2, 2, depth) + tail, low),
        pltpu.VMEM((chunks, 2, depth) + tail, low),
        pltpu.VMEM((chunks, 2, depth - 1) + tail, low),
    ]
    whole = pltpu.VMEM((chunks, 2, 2, 2, 2, depth) + tail, low)
    table = pltpu.VMEM((4, cells // 2, cells // 2), low)
    copies = 3 * chunks * 2 * (3 + depth - 1)
    vmem = pl.BlockSpec(memory_space=pltpu.VMEM)
    hbm = pl.BlockSpec(memory_space=pl.ANY)
    out = jax.ShapeDtypeStruct((strip, 2 * cells), jnp.float32)
    return pl.pallas_call(
        functools.partial(sweep_kernel, depth, scale),
        out_shape=(out, out),
        in_specs=[vmem, vmem, vmem, hbm, hbm],
        out_specs=(vmem, vmem),
        scratch_shapes=[pltpu.VMEM((cells, 2 * cells), low)] * 2
        + [whole] + received + [whole] + received
        + [whole, pltpu.VMEM((CHUNKS, 2, cells, width), low), table, table]
        + [
            pltpu.SemaphoreType.DMA((2 * chunks + 1,)),
            pltpu.SemaphoreType.DMA((copies,)),
            pltpu.SemaphoreType.DMA((copies,)),
        ],
        compiler_params=pltpu.CompilerParams(
            collective_id=0, has_side_effects=True, vmem_limit_bytes=60 * 1024 * 1024
        ),
        name="sweep",
    )(row_func, col_func, chirp, back_first, back_second)


def body(in_modes, back_first, back_second):
    mode_dev = in_modes.shape[0]
    cells = back_first.shape[1]
    axes = ("mgroup", "msub")
    devices_all = lax.axis_size("mgroup") * lax.axis_size("msub")
    scale_all = float(mode_dev * devices_all) ** (-0.5)
    herm_table = hermite_table(grid_points(cells))
    row_funcs = pick_funcs(in_modes[:, 0], herm_table)
    col_funcs = pick_funcs(in_modes[:, 1], herm_table)
    depth = lax.axis_size("mgroup") // 2
    if mode_dev == 1 and lax.axis_size("msub") == 4 and depth == 4 and cells % (16 * devices_all) == 0:
        block = cells // 4
        chirp = jnp.stack([part[:block, :block] for part in chirp_parts(cells)])
        return sweep_call(
            row_funcs.T, col_funcs, chirp, back_first[0], back_second[0], devices_all, depth, scale_all
        )
    fields = (row_funcs[:, :, None] * col_funcs[:, None, :]).astype(jnp.bfloat16)
    table = residue_chirp(cells)
    first = intersection_first(back_first, fields).astype(jnp.bfloat16)
    summed = lax.psum_scatter(first, axes, scatter_dimension=0, tiled=True)
    mask_first = soften(summed.astype(jnp.float32) * scale_all)
    full_mask = lax.all_gather(mask_first.astype(jnp.bfloat16), axes, axis=0, tiled=True)
    full_mask = full_mask.astype(jnp.float32)
    real_part, imag_part = 0.0, 0.0
    for mode in range(mode_dev):
        field = fields[mode].astype(jnp.float32)
        real = (full_mask[:, :cells] * field).astype(jnp.bfloat16).astype(jnp.float32)
        imag = (full_mask[:, cells:] * field).astype(jnp.bfloat16).astype(jnp.float32)
        arr_real, arr_imag = propagate_down(*propagate_columns(real, imag, table), table)
        back = back_second[mode].astype(jnp.float32)
        back_real, back_imag = back[:, :cells], back[:, cells:]
        real_part += back_real * arr_real + back_imag * arr_imag
        imag_part += back_imag * arr_real - back_real * arr_imag
    second = jnp.concatenate([real_part, imag_part], axis=1).astype(jnp.bfloat16)
    summed_two = lax.psum_scatter(second, axes, scatter_dimension=0, tiled=True)
    mask_second = soften(summed_two.astype(jnp.float32) * scale_all)
    return (mask_first, mask_second)


def solution(mesh):
    placed = (
        P(("mgroup", "msub"), None),
        P(("mgroup", "msub"), None, None),
        P(("mgroup", "msub"), None, None),
    )
    return jax.shard_map(
        body,
        mesh=mesh,
        in_specs=placed,
        out_specs=(P(("mgroup", "msub"), None), P(("mgroup", "msub"), None)),
        check_vma=False,
    )
```

time: 416 us -> 111 us (0.27); the launches traced: 408 us -> 111 us
  waiting for transfers between devices: 248 us -> 0 us
  Pallas kernels: 0 us -> 96.1 us
  other arithmetic: 70.3 us -> 5.78 us
  matrix products: 59.2 us -> 3.43 us
  between operations: 14.4 us -> 0.67 us
  local copies, waits for them, and re-layouts: 16.3 us -> 4.9 us
    psum x1 -> x0, waiting for transfers between devices: 133 us -> none  [body(): summed = lax.psum(intersection_first(back_rows, fields), ('mgroup', 'msub'))]
    pallas_call x0 -> x1, Pallas kernels: none -> 96.1 us  [sweep_call(): pl.pallas_call(functools.partial(sweep_kernel, depth, scale), out_shape=(...]
    reduce_scatter x1 -> x0, waiting for transfers between devices: 89.8 us -> none  [body(): lax.psum_scatter(intersection_conj(back_rows, arrived, cells), 'mgroup',...]
    dot_general x3 -> x0, matrix products: 57.6 us -> none  [the longest x1 22.1 us: body(): jnp.einsum('rk,mkc->mrc', chirp_real, spread, preferred_element_type=jnp....]
    convert_element_type x4 -> x0, other arithmetic: 25.5 us -> none  [the longest x1 18.1 us: chirp_parts(): (jnp.sin(phase) * factor).astype(jnp.bfloat16)]
    unnamed x4 -> x0, waiting for transfers between devices: 24.7 us -> none
    neg x2 -> x0, other arithmetic: 19.4 us -> none  [the longest x1 16.7 us: body(): -chirp_imag]
    unnamed x12 -> x2, local copies, waits for them, and re-layouts: 13 us -> 3.34 us
  transfers between devices with their start and end apart: 3 -> 0, of which waited for: 3 -> 0; matrix products, arithmetic and copies ran while one was open for 12% -> 0% of each run, Pallas kernels for 0% -> 0%
where the time goes in v1:
time: 111 us
  Pallas kernels  96.1 us (87%)
  other arithmetic  5.78 us (5%)
  local copies, waits for them, and re-layouts  4.9 us (4%)
  matrix products  3.43 us (3%)
    pallas_call x1, Pallas kernels, sweep_call(): pl.pallas_call(functools.partial(sweep_kernel, depth, scale), out_shape=(...  96.1 us
    dot_general x2, matrix products, pick_funcs(): return jnp.dot(one_hot, herm_table, precision=lax.Precision.HIGHEST)  3.43 us
    unnamed x2, local copies, waits for them, and re-layouts  3.34 us

profile of v1, /device:TPU:0, one launch (start us, length us, event | category | flops | bytes accessed | tf_op | source)
XLA Modules:
  0.0 110.9 jit_solution(3601975445780288450)
XLA Ops:
  0.6 1.3 %fusion.15 = (s32[1,1]{1,0:T(1,128)}, s32[1,1]{1,0:T(1,128)}) fusion(s32[1,2]{1,0:T(1,128)} %param.3), kind=kLoop, calls=%fused_computation.56 | loop fusion | bytes 16 | tf_op jit(solution)/shard_map/slice | solution.py:437
  2.1 0.1 multiply_subtract_fusion.24
  2.1 0.1 multiply_subtract_fusion.22
  2.2 0.1 multiply_subtract_fusion.20
  2.3 0.1 multiply_subtract_fusion.18
  2.4 0.1 multiply_subtract_fusion.16
  2.5 0.1 multiply_subtract_fusion.14
  2.6 0.1 multiply_subtract_fusion.12
  2.7 0.1 multiply_subtract_fusion.10
  2.9 0.1 multiply_subtract_fusion.8
  3.0 0.2 multiply_subtract_fusion.6
  3.2 0.2 multiply_subtract_fusion.4
  3.3 0.2 multiply_subtract_fusion.2
  3.5 0.2 multiply_subtract_fusion
  3.7 0.2 stack.8
  3.9 1.4 %fusion.6.col_ref = f32[1,1024]{1,0:T(1,128)} fusion(f32[32,1024]{1,0:T(8,128)S(1)} %stack.8, s32[]{:T(128)} %bitcast.4), kind=kOutput, calls=%fused_computation.47 | convolution fusion | flops 393248 | bytes 135172 | tf_op jit(solution)/shard_map/dot_general | solution.py:60
  5.3 2.0 %convolution_bitcast_fusion.row_ref = f32[1024,1]{1,0:T(8,128)} fusion(f32[32,1024]{1,0:T(8,128)S(1)} %stack.8, s32[]{:T(128)} %bitcast), kind=kOutput, calls=%fused_computation.6 | convolution fusion | flops 393248 | bytes 135172 | tf_op jit(solution)/shard_map/dot_general | solution.py:60
  7.4 2.1 %fusion.2 = f32[1024,1024]{1,0:T(8,128)S(1)} fusion(), kind=kLoop, calls=%fused_computation.5 | loop fusion | flops 15728640 | bytes 4194304 | tf_op jit(solution)/shard_map/mul | solution.py:40
  9.5 1.2 %fusion.3 = (bf16[1,256,256]{2,1,0:T(8,128)(2,1)S(1)}, bf16[1,256,256]{2,1,0:T(8,128)(2,1)S(1)}) fusion(f32[1024,1024]{1,0:T(8,128)S(1)} %fusion.2), kind=kLoop, calls=%fused_computation.10 | loop fusion | flops 262144 | bytes 524288 | tf_op jit(solution)/shard_map/stack | solution.py:441
  10.7 0.7 pad_maximum_fusion.chirp_ref
  11.4 96.1 %sweep.1 = (f32[32,2048]{1,0:T(8,128)}, f32[32,2048]{1,0:T(8,128)}) custom-call(f32[1024,1]{1,0:T(8,128)} %convolution_bitcast_fusion.row_ref, f32[1,1024]{1,0:T(1,128)} %fusion.6.col_ref, bf16[2,256,256]{2,1,0:T(8,128)(2,1)} %pad_maximum_fusion.chirp_ref, bf16[1024,2048]{1,0:T(8,128)(2,1)} %bitcast.21, bf16[1024,2048]{1,0:T(8,128)(2,1)} %bitcast.22), custom_call_target="tpu_custom_call" | custom-call | tf_op jit(solution)/shard_map/sweep/pallas_call | solution.py:409
  107.6 1.7 %copy.8 = f32[32,2048]{1,0:T(8,128)} copy(f32[32,2048]{1,0:T(8,128)} %get-tuple-element.40) | data formatting | bytes 524288
  109.2 1.7 %copy.9 = f32[32,2048]{1,0:T(8,128)} copy(f32[32,2048]{1,0:T(8,128)} %get-tuple-element.41) | data formatting | bytes 524288
  (3 shorter events, 0.1 us)

commit v2 on v1

--- a/solution.py
+++ b/solution.py
@@ -122,16 +122,16 @@
 
 MESH = pl.DeviceIdType.MESH
 CHUNKS = 4
-OFFSETS = (0, 1, 3, 4, 5, 6, 7, 8, 9)
+OFFSETS = (0, 1, 3, 4, 5, 6, 7, 9, 10)
 OFFSETS_TWO = (0, 1, 2, 3, 4)
 
 
 def sweep_kernel(
     depth, scale,
-    row_ref, col_ref, chirp_ref, first_hbm, second_hbm, out_one, out_two,
+    modes_ref, first_hbm, second_hbm, out_one, out_two,
     first, second, sums, from_core, from_near, from_far, from_z,
     sums2, from_core2, from_near2, from_far2, from_z2,
-    mask, spread, table_col, table_row, local_sem, send_sem, recv_sem,
+    mask, applied, spread, table_col, table_row, row_ref, col_ref, local_sem, send_sem, recv_sem,
 ):
     cells = first.shape[0]
     chunks, strip, width = sums.shape[0], sums.shape[6], sums.shape[7]
@@ -162,6 +162,23 @@
             load(("first", k, h), first_hbm.at[:, at], first.at[:, at])
     load("second", second_hbm, second)
 
+    lanes = row_ref.shape[1]
+    index = lax.broadcasted_iota(jnp.int32, (8, cells), 1).astype(jnp.float32)
+    points = (index - cells / 2 + 0.5) * (span_width / cells)
+    orders = modes_ref[...]
+    row_order, col_order = orders[0:1], orders[1:2]
+    before, current = jnp.zeros_like(points), math.pi ** (-0.25) * jnp.exp(-0.5 * points * points)
+    row_func, col_func = before, before
+    for order in range(ORDERS):
+        row_func = jnp.where(row_order == order, current, row_func)
+        col_func = jnp.where(col_order == order, current, col_func)
+        before, current = current, (
+            math.sqrt(2.0 / (order + 1)) * points * current
+            - math.sqrt(order / (order + 1.0)) * before
+        )
+    col_ref[...] = col_func[:1]
+    row_ref[...] = jnp.broadcast_to(row_func[:1], (lanes, cells)).T
+
     pl.semaphore_wait(barrier, 2 + depth)
 
     sent = []
@@ -177,7 +194,8 @@
 
     def field_at(start, rows, k):
         col = col_ref[:, k * width : (k + 1) * width]
-        return (row_ref[pl.ds(start, rows), :] * col).astype(jnp.bfloat16).astype(jnp.float32)
+        row = jnp.concatenate([row_ref[pl.ds(start, rows), :]] * (width // lanes), axis=1)
+        return (row * col).astype(jnp.bfloat16).astype(jnp.float32)
 
     def soften_pair(real, imag):
         factor = lax.rsqrt(real * real + imag * imag + 1.0)
@@ -294,6 +312,19 @@
         for h in range(2):
             arrivals["g", 3, k, h].wait_recv()
 
+        @pl.loop(0, depth)
+        def _(zz):
+            for cc in range(2):
+                for yy in range(2):
+                    for xx in range(2):
+                        start = pl.multiple_of((((zz * 2 + cc) * 2 + yy) * 2 + xx) * strip, strip)
+                        field = field_at(start, strip, k)
+                        for h in range(2):
+                            a, b = ((xx, yy), (yy, xx))[h]
+                            applied[k, h, pl.ds(start, strip), :] = low(
+                                wide(mask[k, h, cc, a, b, zz]) * field
+                            )
+
     def schedule(stages, offsets, between=None):
         order = sorted(
             (offsets[s] + k, -s, k) for s in range(len(stages)) for k in range(chunks)
@@ -306,7 +337,10 @@
     def build_tables():
         one = lax.broadcasted_iota(jnp.int32, (quarter, quarter), 0)
         two = lax.broadcasted_iota(jnp.int32, (quarter, quarter), 1)
-        real, imag = wide(chirp_ref[0]), wide(chirp_ref[1])
+        square = lax.rem((one - two) * (one - two), 2 * cells)
+        phase = square.astype(jnp.float32) * (math.pi / cells)
+        factor = cells ** (-0.5)
+        real, imag = wide(low(jnp.cos(phase) * factor)), wide(low(jnp.sin(phase) * factor))
         for table, diff, sign in ((table_col, two - one, 1.0), (table_row, one - two, -1.0)):
             for r in range(4):
                 keep = (diff & 3) == r
@@ -325,18 +359,9 @@
     @pl.loop(0, depth)
     def _(zz):
         start = pl.multiple_of(zz * block, block)
-        sides = [[], []]
-        for q in range(4):
-            field = field_at(start, block, q)
-            for h in range(2):
-                strips = []
-                for cc in range(2):
-                    for yy in range(2):
-                        for xx in range(2):
-                            a, b = ((xx, yy), (yy, xx))[h]
-                            strips.append(wide(mask[q, h, cc, a, b, zz]))
-                value = jnp.concatenate(strips, axis=0) * field
-                sides[h].append(wide(low(value)))
+        sides = [
+            [wide(applied[q, h, pl.ds(start, block), :]) for q in range(4)] for h in range(2)
+        ]
         outs = []
         for r, pair in enumerate(four_sums(sides[0], sides[1], -1.0)):
             both = low(jnp.concatenate(pair, axis=1))
@@ -389,7 +414,18 @@
         copy.wait_send()
 
 
-def sweep_call(row_func, col_func, chirp, back_first, back_second, devices, depth, scale):
+def hand_on_kernel(one_in, two_in, one_out, two_out, sem):
+    copies = [
+        pltpu.make_async_copy(one_in, one_out, sem.at[0]),
+        pltpu.make_async_copy(two_in, two_out, sem.at[1]),
+    ]
+    for copy in copies:
+        copy.start()
+    for copy in copies:
+        copy.wait()
+
+
+def sweep_call(modes, back_first, back_second, devices, depth, scale):
     cells = back_first.shape[0]
     strip, width, chunks = cells // devices, cells // CHUNKS, CHUNKS
     low = jnp.bfloat16
@@ -406,14 +442,15 @@
     vmem = pl.BlockSpec(memory_space=pltpu.VMEM)
     hbm = pl.BlockSpec(memory_space=pl.ANY)
     out = jax.ShapeDtypeStruct((strip, 2 * cells), jnp.float32)
-    return pl.pallas_call(
+    swept = pl.pallas_call(
         functools.partial(sweep_kernel, depth, scale),
         out_shape=(out, out),
-        in_specs=[vmem, vmem, vmem, hbm, hbm],
+        in_specs=[vmem, hbm, hbm],
         out_specs=(vmem, vmem),
         scratch_shapes=[pltpu.VMEM((cells, 2 * cells), low)] * 2
         + [whole] + received + [whole] + received
-        + [whole, pltpu.VMEM((CHUNKS, 2, cells, width), low), table, table]
+        + [whole] + [pltpu.VMEM((CHUNKS, 2, cells, width), low)] * 2 + [table, table]
+        + [pltpu.VMEM((cells, 128), jnp.float32), pltpu.VMEM((1, cells), jnp.float32)]
         + [
             pltpu.SemaphoreType.DMA((2 * chunks + 1,)),
             pltpu.SemaphoreType.DMA((copies,)),
@@ -423,7 +460,16 @@
             collective_id=0, has_side_effects=True, vmem_limit_bytes=60 * 1024 * 1024
         ),
         name="sweep",
-    )(row_func, col_func, chirp, back_first, back_second)
+    )(modes, back_first, back_second)
+    return pl.pallas_call(
+        hand_on_kernel,
+        out_shape=(out, out),
+        in_specs=[hbm, hbm],
+        out_specs=(hbm, hbm),
+        scratch_shapes=[pltpu.SemaphoreType.DMA((2,))],
+        compiler_params=pltpu.CompilerParams(vmem_limit_bytes=63 * 1024 * 1024),
+        name="hand_on",
+    )(*swept)
 
 
 def body(in_modes, back_first, back_second):
@@ -432,16 +478,14 @@
     axes = ("mgroup", "msub")
     devices_all = lax.axis_size("mgroup") * lax.axis_size("msub")
     scale_all = float(mode_dev * devices_all) ** (-0.5)
+    depth = lax.axis_size("mgroup") // 2
+    if mode_dev == 1 and lax.axis_size("msub") == 4 and depth == 4 and cells % (16 * devices_all) == 0:
+        return sweep_call(
+            in_modes.T, back_first[0], back_second[0], devices_all, depth, scale_all
+        )
     herm_table = hermite_table(grid_points(cells))
     row_funcs = pick_funcs(in_modes[:, 0], herm_table)
     col_funcs = pick_funcs(in_modes[:, 1], herm_table)
-    depth = lax.axis_size("mgroup") // 2
-    if mode_dev == 1 and lax.axis_size("msub") == 4 and depth == 4 and cells % (16 * devices_all) == 0:
-        block = cells // 4
-        chirp = jnp.stack([part[:block, :block] for part in chirp_parts(cells)])
-        return sweep_call(
-            row_funcs.T, col_funcs, chirp, back_first[0], back_second[0], devices_all, depth, scale_all
-        )
     fields = (row_funcs[:, :, None] * col_funcs[:, None, :]).astype(jnp.bfloat16)
     table = residue_chirp(cells)
     first = intersection_first(back_first, fields).astype(jnp.bfloat16)

time: 111 us -> 115 us (1.036)
  Pallas kernels: 96.1 us -> 113 us
  other arithmetic: 5.78 us -> 0 us
  local copies, waits for them, and re-layouts: 4.9 us -> 1.3 us
  matrix products: 3.43 us -> 0 us
    pallas_call x0 -> x1, Pallas kernels: none -> 17 us  [sweep_call(): pl.pallas_call(hand_on_kernel, out_shape=(out, out), in_specs=[hbm, hbm],...]
    dot_general x2 -> x0, matrix products: 3.43 us -> none  [pick_funcs(): return jnp.dot(one_hot, herm_table, precision=lax.Precision.HIGHEST)]
    unnamed x2 -> x0, local copies, waits for them, and re-layouts: 3.34 us -> none
    mul x2 -> x0, other arithmetic: 2.18 us -> none  [the longest x1 2.15 us: chirp_parts(): phase = square.astype(jnp.float32) * (math.pi / cells)]
    another operation x2 -> x0, other arithmetic: 1.9 us -> none  [body(): chirp = jnp.stack([part[:block, :block] for part in chirp_parts(cells)])]
    sub x15 -> x0, other arithmetic: 1.7 us -> none  [hermite_table(): math.sqrt(2.0 / (order + 1)) * points * current]
    slice x1 -> x0, local copies, waits for them, and re-layouts: 1.31 us -> none  [body(): col_funcs = pick_funcs(in_modes[:, 1], herm_table)]
    transpose x0 -> x1, local copies, waits for them, and re-layouts: none -> 1.3 us  [body(): return sweep_call(in_modes.T, back_first[0], back_second[0], devices_all,...]
where the time goes in v2:
time: 115 us
  Pallas kernels  113 us (98%)
  local copies, waits for them, and re-layouts  1.3 us (1%)
    pallas_call x1, Pallas kernels, sweep_call(): pl.pallas_call(functools.partial(sweep_kernel, depth, scale), out_shape=(...  96.2 us
    pallas_call x1, Pallas kernels, sweep_call(): pl.pallas_call(hand_on_kernel, out_shape=(out, out), in_specs=[hbm, hbm],...  17 us

profile of v2, /device:TPU:0, one launch (start us, length us, event | category | flops | bytes accessed | tf_op | source)
XLA Modules:
  0.0 115.1 jit_solution(16562355370451242742)
XLA Ops:
  0.6 1.3 %copy.5.modes_ref = s32[2,1]{1,0:T(2,128)} copy(s32[2,1]{0,1:T(1,128)} %bitcast.5) | data formatting | bytes 16 | tf_op jit(solution)/shard_map/transpose | solution.py:484
  1.9 96.2 %sweep.1 = (f32[32,2048]{1,0:T(8,128)}, f32[32,2048]{1,0:T(8,128)}) custom-call(s32[2,1]{1,0:T(2,128)} %copy.5.modes_ref, bf16[1024,2048]{1,0:T(8,128)(2,1)} %bitcast.3, bf16[1024,2048]{1,0:T(8,128)(2,1)} %bitcast.4), custom_call_target="tpu_custom_call" | custom-call | tf_op jit(solution)/shard_map/sweep/pallas_call | solution.py:445
  98.1 17.0 %hand_on.1 = (f32[32,2048]{1,0:T(8,128)}, f32[32,2048]{1,0:T(8,128)}) custom-call(f32[32,2048]{1,0:T(8,128)} %get-tuple-element.4.one_in, f32[32,2048]{1,0:T(8,128)} %get-tuple-element.5.two_in), custom_call_target="tpu_custom_call" | custom-call | tf_op jit(solution)/shard_map/hand_on/pallas_call | solution.py:464

commit v3 on v2

--- a/solution.py
+++ b/solution.py
@@ -121,9 +121,12 @@
 
 
 MESH = pl.DeviceIdType.MESH
-CHUNKS = 4
-OFFSETS = (0, 1, 3, 4, 5, 6, 7, 9, 10)
-OFFSETS_TWO = (0, 1, 2, 3, 4)
+CHUNKS = 8
+KEYS = (
+    (0.3, 0.7), (1.1, 0.9), (2.8, 0.9), (3.7, 1.0), (5.2, 1.0),
+    (7.0, 0.9), (8.9, 0.8), (11.5, 0.8), (12.7, 1.1),
+)
+KEYS_TWO = ((0.0, 0.5), (1.4, 0.5), (3.3, 0.3), (3.9, 0.3), (22.7, 6.4))
 
 
 def sweep_kernel(
@@ -137,6 +140,7 @@
     chunks, strip, width = sums.shape[0], sums.shape[6], sums.shape[7]
     block = cells // depth
     quarter = cells // 4
+    pieces = quarter // width
     group, sub = lax.axis_index("mgroup"), lax.axis_index("msub")
     z, c = group // 2, group % 2
     y, x = sub // 2, sub % 2
@@ -166,7 +170,7 @@
     index = lax.broadcasted_iota(jnp.int32, (8, cells), 1).astype(jnp.float32)
     points = (index - cells / 2 + 0.5) * (span_width / cells)
     orders = modes_ref[...]
-    row_order, col_order = orders[0:1], orders[1:2]
+    row_order, col_order = orders[:, 0:1], orders[:, 1:2]
     before, current = jnp.zeros_like(points), math.pi ** (-0.25) * jnp.exp(-0.5 * points * points)
     row_func, col_func = before, before
     for order in range(ORDERS):
@@ -311,6 +315,7 @@
     def gather_done(k):
         for h in range(2):
             arrivals["g", 3, k, h].wait_recv()
+        piece = pl.ds(k % pieces * width, width)
 
         @pl.loop(0, depth)
         def _(zz):
@@ -321,18 +326,22 @@
                         field = field_at(start, strip, k)
                         for h in range(2):
                             a, b = ((xx, yy), (yy, xx))[h]
-                            applied[k, h, pl.ds(start, strip), :] = low(
+                            applied[k // pieces, h, pl.ds(start, strip), piece] = low(
                                 wide(mask[k, h, cc, a, b, zz]) * field
                             )
 
-    def schedule(stages, offsets, between=None):
+    def schedule(stages, keys, between=None):
         order = sorted(
-            (offsets[s] + k, -s, k) for s in range(len(stages)) for k in range(chunks)
+            (keys[s][0] + keys[s][1] * k, -s, k) for s in range(len(stages)) for k in range(chunks)
         )
-        for n, (_, s, k) in enumerate(order):
-            if between and n == 2 * chunks:
+        waiting, done = [(-s, k) for _, s, k in order], []
+        while waiting:
+            s, k = next((s, k) for s, k in waiting if s == 0 or (s - 1, k) in done)
+            waiting.remove((s, k))
+            done.append((s, k))
+            if between and len(done) == 2 * chunks:
                 between()
-            stages[-s](k)
+            stages[s](k)
 
     def build_tables():
         one = lax.broadcasted_iota(jnp.int32, (quarter, quarter), 0)
@@ -353,7 +362,7 @@
 
     schedule(
         (product, near_send, far_send, z_send, first_mask, gather_far, gather_near, gather_core, gather_done),
-        OFFSETS, build_tables,
+        KEYS, build_tables,
     )
 
     @pl.loop(0, depth)
@@ -378,8 +387,10 @@
     def arrive(k):
         if k == 0:
             loads["second"].wait()
+        piece = pl.ds(k % pieces * width, width)
         sides = [
-            [wide(spread[k, h, q * quarter : (q + 1) * quarter, :]) for q in range(4)] for h in range(2)
+            [wide(spread[k // pieces, h, q * quarter : (q + 1) * quarter, piece]) for q in range(4)]
+            for h in range(2)
         ]
         outs = []
         for r, pair in enumerate(four_sums(sides[0], sides[1], -1.0)):
@@ -409,20 +420,14 @@
         out_two[:, k * width : (k + 1) * width] = real
         out_two[:, cells + k * width : cells + (k + 1) * width] = imag
 
-    schedule((arrive, near_send2, far_send2, z_send2, second_mask), OFFSETS_TWO)
+    schedule((arrive, near_send2, far_send2, z_send2, second_mask), KEYS_TWO)
     for copy in sent:
         copy.wait_send()
 
 
-def hand_on_kernel(one_in, two_in, one_out, two_out, sem):
-    copies = [
-        pltpu.make_async_copy(one_in, one_out, sem.at[0]),
-        pltpu.make_async_copy(two_in, two_out, sem.at[1]),
-    ]
-    for copy in copies:
-        copy.start()
-    for copy in copies:
-        copy.wait()
+def hand_on_kernel(one_in, two_in, one_out, two_out):
+    one_out[...] = one_in[...]
+    two_out[...] = two_in[...]
 
 
 def sweep_call(modes, back_first, back_second, devices, depth, scale):
@@ -449,7 +454,7 @@
         out_specs=(vmem, vmem),
         scratch_shapes=[pltpu.VMEM((cells, 2 * cells), low)] * 2
         + [whole] + received + [whole] + received
-        + [whole] + [pltpu.VMEM((CHUNKS, 2, cells, width), low)] * 2 + [table, table]
+        + [whole] + [pltpu.VMEM((4, 2, cells, cells // 4), low)] * 2 + [table, table]
         + [pltpu.VMEM((cells, 128), jnp.float32), pltpu.VMEM((1, cells), jnp.float32)]
         + [
             pltpu.SemaphoreType.DMA((2 * chunks + 1,)),
@@ -464,9 +469,8 @@
     return pl.pallas_call(
         hand_on_kernel,
         out_shape=(out, out),
-        in_specs=[hbm, hbm],
-        out_specs=(hbm, hbm),
-        scratch_shapes=[pltpu.SemaphoreType.DMA((2,))],
+        in_specs=[vmem, vmem],
+        out_specs=(vmem, vmem),
         compiler_params=pltpu.CompilerParams(vmem_limit_bytes=63 * 1024 * 1024),
         name="hand_on",
     )(*swept)
@@ -479,9 +483,9 @@
     devices_all = lax.axis_size("mgroup") * lax.axis_size("msub")
     scale_all = float(mode_dev * devices_all) ** (-0.5)
     depth = lax.axis_size("mgroup") // 2
-    if mode_dev == 1 and lax.axis_size("msub") == 4 and depth == 4 and cells % (16 * devices_all) == 0:
+    if mode_dev == 1 and lax.axis_size("msub") == 4 and depth == 4 and cells % (16 * devices_all) == cells % (128 * CHUNKS) == 0:
         return sweep_call(
-            in_modes.T, back_first[0], back_second[0], devices_all, depth, scale_all
+            in_modes, back_first[0], back_second[0], devices_all, depth, scale_all
         )
     herm_table = hermite_table(grid_points(cells))
     row_funcs = pick_funcs(in_modes[:, 0], herm_table)

time: 115 us -> 91 us (0.79)
  Pallas kernels: 113 us -> 90.2 us
  local copies, waits for them, and re-layouts: 1.3 us -> 0 us
    pallas_call x1, Pallas kernels: 17 us -> 1.84 us  [sweep_call(): pl.pallas_call(hand_on_kernel, out_shape=(out, out), in_specs=[vmem, vmem...]
    pallas_call x1, Pallas kernels: 96.2 us -> 88.4 us  [sweep_call(): pl.pallas_call(functools.partial(sweep_kernel, depth, scale), out_shape=(...]
    transpose x1 -> x0, local copies, waits for them, and re-layouts: 1.3 us -> none  [body(): return sweep_call(in_modes.T, back_first[0], back_second[0], devices_all,...]
where the time goes in v3:
time: 91 us; the launch traced here: 90.9 us
  Pallas kernels  90.2 us (99%)
    pallas_call x1, Pallas kernels, sweep_call(): pl.pallas_call(functools.partial(sweep_kernel, depth, scale), out_shape=(...  88.4 us
    pallas_call x1, Pallas kernels, sweep_call(): pl.pallas_call(hand_on_kernel, out_shape=(out, out), in_specs=[vmem, vmem...  1.84 us

profile of v3, /device:TPU:0, one launch (start us, length us, event | category | flops | bytes accessed | tf_op | source)
XLA Modules:
  0.0 90.9 jit_solution(11891162557608369345)
XLA Ops:
  0.6 88.4 %sweep.1 = (f32[32,2048]{1,0:T(8,128)}, f32[32,2048]{1,0:T(8,128)}) custom-call(s32[1,2]{1,0:T(1,128)} %modes_ref.1, bf16[1024,2048]{1,0:T(8,128)(2,1)} %bitcast.2, bf16[1024,2048]{1,0:T(8,128)(2,1)} %bitcast.3), custom_call_target="tpu_custom_call" | custom-call | tf_op jit(solution)/shard_map/sweep/pallas_call | solution.py:450
  89.0 1.8 %hand_on.1 = (f32[32,2048]{1,0:T(8,128)}, f32[32,2048]{1,0:T(8,128)}) custom-call(f32[32,2048]{1,0:T(8,128)} %get-tuple-element.4.one_in, f32[32,2048]{1,0:T(8,128)} %get-tuple-element.5.two_in), custom_call_target="tpu_custom_call" | custom-call | tf_op jit(solution)/shard_map/hand_on/pallas_call | solution.py:469

commit v4 on v3

--- a/solution.py
+++ b/solution.py
@@ -83,7 +83,8 @@
     even_r, even_i = real[0] + real[2], imag[0] + imag[2]
     odd_r, odd_i = real[1] + real[3], imag[1] + imag[3]
     low_r, low_i = real[0] - real[2], imag[0] - imag[2]
-    top_r, top_i = sign * (real[1] - real[3]), sign * (imag[1] - imag[3])
+    one, three = (1, 3) if sign > 0 else (3, 1)
+    top_r, top_i = real[one] - real[three], imag[one] - imag[three]
     return (
         (even_r + odd_r, even_i + odd_i),
         (low_r - top_i, low_i + top_r),
@@ -134,13 +135,14 @@
     modes_ref, first_hbm, second_hbm, out_one, out_two,
     first, second, sums, from_core, from_near, from_far, from_z,
     sums2, from_core2, from_near2, from_far2, from_z2,
-    mask, applied, spread, table_col, table_row, row_ref, col_ref, local_sem, send_sem, recv_sem,
+    mask, applied, spread, partial, table_col, table_row, row_ref, col_ref, local_sem, send_sem, recv_sem,
 ):
     cells = first.shape[0]
     chunks, strip, width = sums.shape[0], sums.shape[6], sums.shape[7]
     block = cells // depth
     quarter = cells // 4
     pieces = quarter // width
+    column = [k % 4 * quarter + k // 4 * width for k in range(chunks)]
     group, sub = lax.axis_index("mgroup"), lax.axis_index("msub")
     z, c = group // 2, group % 2
     y, x = sub // 2, sub % 2
@@ -162,7 +164,7 @@
         loads[name] = copy
     for k in range(chunks):
         for h in range(2):
-            at = pl.ds(h * cells + k * width, width)
+            at = pl.ds(h * cells + column[k], width)
             load(("first", k, h), first_hbm.at[:, at], first.at[:, at])
     load("second", second_hbm, second)
 
@@ -183,8 +185,6 @@
     col_ref[...] = col_func[:1]
     row_ref[...] = jnp.broadcast_to(row_func[:1], (lanes, cells)).T
 
-    pl.semaphore_wait(barrier, 2 + depth)
-
     sent = []
     def send(src, dst, peer):
         at = len(sent)
@@ -197,9 +197,9 @@
         return copy
 
     def field_at(start, rows, k):
-        col = col_ref[:, k * width : (k + 1) * width]
+        col = col_ref[:, column[k] : column[k] + width]
         row = jnp.concatenate([row_ref[pl.ds(start, rows), :]] * (width // lanes), axis=1)
-        return (row * col).astype(jnp.bfloat16).astype(jnp.float32)
+        return (row * col).astype(jnp.bfloat16)
 
     def soften_pair(real, imag):
         factor = lax.rsqrt(real * real + imag * imag + 1.0)
@@ -211,24 +211,23 @@
 
     def reduce_stages(tag, acc, rc, rn, rf, rz):
         def core_send(k):
+            arrivals[tag, 0, k] = send(acc.at[k, 1 - c], rc.at[k], sibling)
+
+        def near_send(k):
+            arrivals[tag, 0, k].wait_recv()
             for h in range(2):
-                arrivals[tag, 0, k, h] = send(acc.at[k, h, 1 - c], rc.at[k, h], sibling)
-
-        def near_send(k):
-            for h in range(2):
-                arrivals[tag, 0, k, h].wait_recv()
                 a = 1 - near[h]
-                acc[k, h, c, a] = low(wide(acc[k, h, c, a]) + wide(rc[k, h, a]))
-                arrivals[tag, 1, k, h] = send(acc.at[k, h, c, a], rn.at[k, h], near_dev[h])
+                acc[k, c, h, a] = acc[k, c, h, a] + rc[k, h, a]
+                arrivals[tag, 1, k, h] = send(acc.at[k, c, h, a], rn.at[k, h], near_dev[h])
 
         def far_send(k):
             for h in range(2):
                 arrivals[tag, 1, k, h].wait_recv()
                 a, b = near[h], 1 - far[h]
-                acc[k, h, c, a, b] = low(
-                    wide(acc[k, h, c, a, b]) + wide(rc[k, h, a, b]) + wide(rn[k, h, b])
+                acc[k, c, h, a, b] = low(
+                    wide(acc[k, c, h, a, b]) + wide(rc[k, h, a, b]) + wide(rn[k, h, b])
                 )
-                arrivals[tag, 2, k, h] = send(acc.at[k, h, c, a, b], rf.at[k, h], far_dev[h])
+                arrivals[tag, 2, k, h] = send(acc.at[k, c, h, a, b], rf.at[k, h], far_dev[h])
 
         def z_send(k):
             for h in range(2):
@@ -236,19 +235,19 @@
                 a, b = near[h], far[h]
                 for i in range(1, depth):
                     to = lax.rem(z + i, depth)
-                    acc[k, h, c, a, b, to] = low(
-                        wide(acc[k, h, c, a, b, to]) + wide(rc[k, h, a, b, to])
+                    acc[k, c, h, a, b, to] = low(
+                        wide(acc[k, c, h, a, b, to]) + wide(rc[k, h, a, b, to])
                         + wide(rn[k, h, b, to]) + wide(rf[k, h, to])
                     )
                     arrivals[tag, 3, k, h, i] = send(
-                        acc.at[k, h, c, a, b, to], rz.at[k, h, i - 1], along_z[i - 1]
+                        acc.at[k, c, h, a, b, to], rz.at[k, h, i - 1], along_z[i - 1]
                     )
 
         def finish(k):
             totals = []
             for h in range(2):
                 a, b = near[h], far[h]
-                total = wide(acc[k, h, c, a, b, z]) + wide(rc[k, h, a, b, z])
+                total = wide(acc[k, c, h, a, b, z]) + wide(rc[k, h, a, b, z])
                 total += wide(rn[k, h, b, z]) + wide(rf[k, h, z])
                 for i in range(1, depth):
                     arrivals[tag, 3, k, h, i].wait_recv()
@@ -273,49 +272,48 @@
                         start = pl.multiple_of((((zz * 2 + part) * 2 + yy) * 2 + xx) * strip, strip)
                         field = field_at(start, strip, k)
                         for h in range(2):
-                            at = h * cells + k * width
-                            value = wide(first[pl.ds(start, strip), at : at + width]) * field
+                            at = h * cells + column[k]
                             a, b = ((xx, yy), (yy, xx))[h]
-                            sums[k, h, part, a, b, zz] = low(value)
+                            sums[k, part, h, a, b, zz] = first[pl.ds(start, strip), at : at + width] * field
         half(1 - c)
+        if k == 0:
+            pl.semaphore_wait(barrier, 2 + depth)
         core_send(k)
         half(c)
 
     def first_mask(k):
         real, imag = finish(k)
         for h, value in enumerate((real, imag)):
-            at = h * cells + k * width
+            at = h * cells + column[k]
             out_one[:, at : at + width] = value
             a, b = near[h], far[h]
-            mask[k, h, c, a, b, z] = low(value)
+            mask[k, c, h, a, b, z] = low(value)
             for i in range(1, depth):
                 arrivals["g", 0, k, h, i] = send(
-                    mask.at[k, h, c, a, b, z], mask.at[k, h, c, a, b, z], along_z[i - 1]
+                    mask.at[k, c, h, a, b, z], mask.at[k, c, h, a, b, z], along_z[i - 1]
                 )
 
     def gather_far(k):
         for h in range(2):
             for i in range(1, depth):
                 arrivals["g", 0, k, h, i].wait_recv()
-            at = mask.at[k, h, c, near[h], far[h]]
+            at = mask.at[k, c, h, near[h], far[h]]
             arrivals["g", 1, k, h] = send(at, at, far_dev[h])
 
     def gather_near(k):
         for h in range(2):
             arrivals["g", 1, k, h].wait_recv()
-            at = mask.at[k, h, c, near[h]]
+            at = mask.at[k, c, h, near[h]]
             arrivals["g", 2, k, h] = send(at, at, near_dev[h])
 
     def gather_core(k):
         for h in range(2):
             arrivals["g", 2, k, h].wait_recv()
-            at = mask.at[k, h, c]
-            arrivals["g", 3, k, h] = send(at, at, sibling)
+        at = mask.at[k, c]
+        arrivals["g", 3, k] = send(at, at, sibling)
 
     def gather_done(k):
-        for h in range(2):
-            arrivals["g", 3, k, h].wait_recv()
-        piece = pl.ds(k % pieces * width, width)
+        arrivals["g", 3, k].wait_recv()
 
         @pl.loop(0, depth)
         def _(zz):
@@ -326,9 +324,31 @@
                         field = field_at(start, strip, k)
                         for h in range(2):
                             a, b = ((xx, yy), (yy, xx))[h]
-                            applied[k // pieces, h, pl.ds(start, strip), piece] = low(
-                                wide(mask[k, h, cc, a, b, zz]) * field
-                            )
+                            applied[k, h, pl.ds(start, strip), :] = mask[k, cc, h, a, b, zz] * field
+
+    def columns_part(zz, part):
+        start = pl.multiple_of(zz * block, block)
+        sides = [
+            [applied[part * 4 + q, h, pl.ds(start, block), :] for q in range(4)] for h in range(2)
+        ]
+        for r, pair in enumerate(four_sums(sides[0], sides[1], -1)):
+            both = jnp.concatenate(pair, axis=1)
+            rows = slice(part * 2 * width, (part + 1) * 2 * width)
+            out = jnp.dot(both, table_col[r, rows], preferred_element_type=jnp.float32)
+            if part > 0:
+                out += partial[r, pl.ds(start, block), :]
+            if part < pieces - 1:
+                partial[r, pl.ds(start, block), :] = out
+            else:
+                yield out
+
+    def early_columns(k):
+        gather_done(k)
+        for zz in range(depth):
+            part, last = divmod(k - zz - 3, 4)
+            if last == 0 and 0 <= part < pieces - 1:
+                for _ in columns_part(zz, part):
+                    pass
 
     def schedule(stages, keys, between=None):
         order = sorted(
@@ -350,31 +370,32 @@
         phase = square.astype(jnp.float32) * (math.pi / cells)
         factor = cells ** (-0.5)
         real, imag = wide(low(jnp.cos(phase) * factor)), wide(low(jnp.sin(phase) * factor))
-        for table, diff, sign in ((table_col, two - one, 1.0), (table_row, one - two, -1.0)):
-            for r in range(4):
-                keep = (diff & 3) == r
-                rr = jnp.where(keep, real, 0.0)
-                ii = jnp.where(keep, imag, 0.0)
-                table[r, :quarter, :quarter] = low(rr)
-                table[r, quarter:, quarter:] = low(rr)
-                table[r, :quarter, quarter:] = low(sign * ii)
-                table[r, quarter:, :quarter] = low(-sign * ii)
+        for r in range(4):
+            keep = ((two - one) & 3) == r
+            rr, ii = low(jnp.where(keep, real, 0.0)), low(jnp.where(keep, imag, 0.0))
+            for n in range(pieces):
+                rows = slice(n * width, (n + 1) * width)
+                to = 2 * n * width
+                table_col[r, to : to + width, :quarter] = rr[rows]
+                table_col[r, to : to + width, quarter:] = ii[rows]
+                table_col[r, to + width : to + 2 * width, :quarter] = -ii[rows]
+                table_col[r, to + width : to + 2 * width, quarter:] = rr[rows]
+            keep = ((one - two) & 3) == r
+            rr, ii = low(jnp.where(keep, real, 0.0)), low(jnp.where(keep, imag, 0.0))
+            table_row[r, :quarter, :quarter] = rr
+            table_row[r, quarter:, quarter:] = rr
+            table_row[r, :quarter, quarter:] = -ii
+            table_row[r, quarter:, :quarter] = ii
 
     schedule(
-        (product, near_send, far_send, z_send, first_mask, gather_far, gather_near, gather_core, gather_done),
+        (product, near_send, far_send, z_send, first_mask, gather_far, gather_near, gather_core, early_columns),
         KEYS, build_tables,
     )
 
     @pl.loop(0, depth)
     def _(zz):
         start = pl.multiple_of(zz * block, block)
-        sides = [
-            [wide(applied[q, h, pl.ds(start, block), :]) for q in range(4)] for h in range(2)
-        ]
-        outs = []
-        for r, pair in enumerate(four_sums(sides[0], sides[1], -1.0)):
-            both = low(jnp.concatenate(pair, axis=1))
-            outs.append(jnp.dot(both, table_col[r], preferred_element_type=jnp.float32))
+        outs = list(columns_part(zz, pieces - 1))
         done = four_sums([o[:, :quarter] for o in outs], [o[:, quarter:] for o in outs], 1.0)
         for p in range(4):
             for h in range(2):
@@ -387,20 +408,20 @@
     def arrive(k):
         if k == 0:
             loads["second"].wait()
-        piece = pl.ds(k % pieces * width, width)
+        piece = pl.ds(k // 4 * width, width)
         sides = [
-            [wide(spread[k // pieces, h, q * quarter : (q + 1) * quarter, piece]) for q in range(4)]
+            [spread[k % 4, h, q * quarter : (q + 1) * quarter, piece] for q in range(4)]
             for h in range(2)
         ]
         outs = []
-        for r, pair in enumerate(four_sums(sides[0], sides[1], -1.0)):
-            both = low(jnp.concatenate(pair, axis=0))
+        for r, pair in enumerate(four_sums(sides[0], sides[1], -1)):
+            both = jnp.concatenate(pair, axis=0)
             outs.append(jnp.dot(table_row[r], both, preferred_element_type=jnp.float32))
         done = four_sums([o[:quarter] for o in outs], [o[quarter:] for o in outs], 1.0)
         for p in range(4):
             rows = slice(p * quarter, (p + 1) * quarter)
-            back_real = wide(second[rows, k * width : (k + 1) * width])
-            back_imag = wide(second[rows, cells + k * width : cells + (k + 1) * width])
+            back_real = wide(second[rows, column[k] : column[k] + width])
+            back_imag = wide(second[rows, cells + column[k] : cells + column[k] + width])
             arr_real, arr_imag = done[p]
             terms = (
                 back_real * arr_real + back_imag * arr_imag,
@@ -412,13 +433,13 @@
                     number = p * (quarter // strip) + n
                     xx, yy, cc, zz = number % 2, number // 2 % 2, number // 4 % 2, number // 8
                     a, b = ((xx, yy), (yy, xx))[h]
-                    sums2[k, h, cc, a, b, zz] = value[n * strip : (n + 1) * strip]
+                    sums2[k, cc, h, a, b, zz] = value[n * strip : (n + 1) * strip]
         core_send2(k)
 
     def second_mask(k):
         real, imag = finish2(k)
-        out_two[:, k * width : (k + 1) * width] = real
-        out_two[:, cells + k * width : cells + (k + 1) * width] = imag
+        out_two[:, column[k] : column[k] + width] = real
+        out_two[:, cells + column[k] : cells + column[k] + width] = imag
 
     schedule((arrive, near_send2, far_send2, z_send2, second_mask), KEYS_TWO)
     for copy in sent:
@@ -454,7 +475,8 @@
         out_specs=(vmem, vmem),
         scratch_shapes=[pltpu.VMEM((cells, 2 * cells), low)] * 2
         + [whole] + received + [whole] + received
-        + [whole] + [pltpu.VMEM((4, 2, cells, cells // 4), low)] * 2 + [table, table]
+        + [whole] + [pltpu.VMEM((chunks, 2, cells, width), low), pltpu.VMEM((4, 2, cells, cells // 4), low)]
+        + [pltpu.VMEM((4, cells, cells // 2), jnp.float32), table, table]
         + [pltpu.VMEM((cells, 128), jnp.float32), pltpu.VMEM((1, cells), jnp.float32)]
         + [
             pltpu.SemaphoreType.DMA((2 * chunks + 1,)),

time: 91 us -> 90.2 us (level)
  no operation moved by 1% of the time
where the time goes in v4:
time: 90.2 us; the launch traced here: 90 us
  Pallas kernels  89.4 us (99%)
    pallas_call x1, Pallas kernels, sweep_call(): pl.pallas_call(functools.partial(sweep_kernel, depth, scale), out_shape=(...  87.5 us
    pallas_call x1, Pallas kernels, sweep_call(): pl.pallas_call(hand_on_kernel, out_shape=(out, out), in_specs=[vmem, vmem...  1.84 us

profile of v4, /device:TPU:0, one launch (start us, length us, event | category | flops | bytes accessed | tf_op | source)
XLA Modules:
  0.0 90.0 jit_solution(13049726739295826262)
XLA Ops:
  0.6 87.5 %sweep.1 = (f32[32,2048]{1,0:T(8,128)}, f32[32,2048]{1,0:T(8,128)}) custom-call(s32[1,2]{1,0:T(1,128)} %modes_ref.1, bf16[1024,2048]{1,0:T(8,128)(2,1)} %bitcast.2, bf16[1024,2048]{1,0:T(8,128)(2,1)} %bitcast.3), custom_call_target="tpu_custom_call" | custom-call | tf_op jit(solution)/shard_map/sweep/pallas_call | solution.py:471
  88.2 1.8 %hand_on.1 = (f32[32,2048]{1,0:T(8,128)}, f32[32,2048]{1,0:T(8,128)}) custom-call(f32[32,2048]{1,0:T(8,128)} %get-tuple-element.4.one_in, f32[32,2048]{1,0:T(8,128)} %get-tuple-element.5.two_in), custom_call_target="tpu_custom_call" | custom-call | tf_op jit(solution)/shard_map/hand_on/pallas_call | solution.py:491

commit v5 on v4

--- a/solution.py
+++ b/solution.py
@@ -123,6 +123,7 @@
 
 MESH = pl.DeviceIdType.MESH
 CHUNKS = 8
+Z_FIRST = 2
 KEYS = (
     (0.3, 0.7), (1.1, 0.9), (2.8, 0.9), (3.7, 1.0), (5.2, 1.0),
     (7.0, 0.9), (8.9, 0.8), (11.5, 0.8), (12.7, 1.1),
@@ -133,8 +134,8 @@
 def sweep_kernel(
     depth, scale,
     modes_ref, first_hbm, second_hbm, out_one, out_two,
-    first, second, sums, from_core, from_near, from_far, from_z,
-    sums2, from_core2, from_near2, from_far2, from_z2,
+    first, second, sums, from_core, from_near, from_far, from_z, z_first,
+    sums2, from_core2, from_near2, from_far2, from_z2, z_first2,
     mask, applied, spread, partial, table_col, table_row, row_ref, col_ref, local_sem, send_sem, recv_sem,
 ):
     cells = first.shape[0]
@@ -209,7 +210,7 @@
     low = lambda value: value.astype(jnp.bfloat16)
     arrivals = {}
 
-    def reduce_stages(tag, acc, rc, rn, rf, rz):
+    def reduce_stages(tag, acc, rc, rn, rf, rz, zf):
         def core_send(k):
             arrivals[tag, 0, k] = send(acc.at[k, 1 - c], rc.at[k], sibling)
 
@@ -255,10 +256,60 @@
                 totals.append(total * scale)
             return soften_pair(*totals)
 
-        return core_send, near_send, far_send, z_send, finish
+        def z_send_first(k):
+            arrivals[tag, 0, k].wait_recv()
+            for h in range(2):
+                for i in range(1, depth):
+                    to = lax.rem(z + i, depth)
+                    acc[k, c, h, :, :, to] = acc[k, c, h, :, :, to] + rc[k, h, :, :, to]
+                    arrivals[tag, 1, k, h, i] = send(
+                        acc.at[k, c, h, :, :, to], zf.at[h, i - 1], along_z[i - 1]
+                    )
+
+        def z_total(k, h, a, b):
+            total = wide(acc[k, c, h, a, b, z]) + wide(rc[k, h, a, b, z])
+            for i in range(1, depth):
+                total += wide(zf[h, i - 1, a, b])
+            return total
+
+        def near_send_second(k):
+            for h in range(2):
+                for i in range(1, depth):
+                    arrivals[tag, 1, k, h, i].wait_recv()
+                a = 1 - near[h]
+                for b in range(2):
+                    acc[k, c, h, a, b, z] = low(z_total(k, h, a, b))
+                arrivals[tag, 2, k, h] = send(acc.at[k, c, h, a, :, z], rn.at[k, h, :, 0], near_dev[h])
+
+        def far_send_last(k):
+            for h in range(2):
+                arrivals[tag, 2, k, h].wait_recv()
+                a, b = near[h], 1 - far[h]
+                acc[k, c, h, a, b, z] = low(z_total(k, h, a, b) + wide(rn[k, h, b, 0]))
+                arrivals[tag, 3, k, h] = send(acc.at[k, c, h, a, b, z], rf.at[k, h, 0], far_dev[h])
+
+        def finish_first(k):
+            totals = []
+            for h in range(2):
+                a, b = near[h], far[h]
+                arrivals[tag, 3, k, h].wait_recv()
+                total = z_total(k, h, a, b) + wide(rn[k, h, b, 0]) + wide(rf[k, h, 0])
+                totals.append(total * scale)
+            return soften_pair(*totals)
+
+        def choose(one, other):
+            return lambda k: other(k) if k == Z_FIRST else one(k)
+
+        return (
+            core_send,
+            choose(near_send, z_send_first),
+            choose(far_send, near_send_second),
+            choose(z_send, far_send_last),
+            choose(finish, finish_first),
+        )
 
     core_send, near_send, far_send, z_send, finish = reduce_stages(
-        1, sums, from_core, from_near, from_far, from_z
+        1, sums, from_core, from_near, from_far, from_z, z_first
     )
 
     def product(k):
@@ -288,27 +339,43 @@
             out_one[:, at : at + width] = value
             a, b = near[h], far[h]
             mask[k, c, h, a, b, z] = low(value)
-            for i in range(1, depth):
-                arrivals["g", 0, k, h, i] = send(
-                    mask.at[k, c, h, a, b, z], mask.at[k, c, h, a, b, z], along_z[i - 1]
-                )
+            at = mask.at[k, c, h, a, b, z]
+            if k == Z_FIRST:
+                arrivals["g", 0, k, h] = send(at, at, far_dev[h])
+            else:
+                for i in range(1, depth):
+                    arrivals["g", 0, k, h, i] = send(at, at, along_z[i - 1])
 
     def gather_far(k):
         for h in range(2):
-            for i in range(1, depth):
-                arrivals["g", 0, k, h, i].wait_recv()
-            at = mask.at[k, c, h, near[h], far[h]]
-            arrivals["g", 1, k, h] = send(at, at, far_dev[h])
+            if k == Z_FIRST:
+                arrivals["g", 0, k, h].wait_recv()
+                at = mask.at[k, c, h, near[h], :, z]
+                arrivals["g", 1, k, h] = send(at, at, near_dev[h])
+            else:
+                for i in range(1, depth):
+                    arrivals["g", 0, k, h, i].wait_recv()
+                at = mask.at[k, c, h, near[h], far[h]]
+                arrivals["g", 1, k, h] = send(at, at, far_dev[h])
 
     def gather_near(k):
         for h in range(2):
             arrivals["g", 1, k, h].wait_recv()
-            at = mask.at[k, c, h, near[h]]
-            arrivals["g", 2, k, h] = send(at, at, near_dev[h])
+            if k == Z_FIRST:
+                at = mask.at[k, c, h, :, :, z]
+                for i in range(1, depth):
+                    arrivals["g", 2, k, h, i] = send(at, at, along_z[i - 1])
+            else:
+                at = mask.at[k, c, h, near[h]]
+                arrivals["g", 2, k, h] = send(at, at, near_dev[h])
 
     def gather_core(k):
         for h in range(2):
-            arrivals["g", 2, k, h].wait_recv()
+            if k == Z_FIRST:
+                for i in range(1, depth):
+                    arrivals["g", 2, k, h, i].wait_recv()
+            else:
+                arrivals["g", 2, k, h].wait_recv()
         at = mask.at[k, c]
         arrivals["g", 3, k] = send(at, at, sibling)
 
@@ -402,7 +469,7 @@
                 spread[p, h, pl.ds(start, block), :] = low(done[p][h])
 
     core_send2, near_send2, far_send2, z_send2, finish2 = reduce_stages(
-        2, sums2, from_core2, from_near2, from_far2, from_z2
+        2, sums2, from_core2, from_near2, from_far2, from_z2, z_first2
     )
 
     def arrive(k):
@@ -461,6 +528,7 @@
         pltpu.VMEM((chunks, 2, 2, depth) + tail, low),
         pltpu.VMEM((chunks, 2, depth) + tail, low),
         pltpu.VMEM((chunks, 2, depth - 1) + tail, low),
+        pltpu.VMEM((2, depth - 1, 2, 2) + tail, low),
     ]
     whole = pltpu.VMEM((chunks, 2, 2, 2, 2, depth) + tail, low)
     table = pltpu.VMEM((4, cells // 2, cells // 2), low)

time: 90.2 us -> 98.4 us (1.091)
  Pallas kernels: 89.4 us -> 97.6 us
    pallas_call x1, Pallas kernels: 87.5 us -> 95.8 us  [sweep_call(): pl.pallas_call(functools.partial(sweep_kernel, depth, scale), out_shape=(...]
where the time goes in v5:
time: 98.4 us; the launch traced here: 98.3 us
  Pallas kernels  97.6 us (99%)
    pallas_call x1, Pallas kernels, sweep_call(): pl.pallas_call(functools.partial(sweep_kernel, depth, scale), out_shape=(...  95.8 us

profile of v5, /device:TPU:0, one launch (start us, length us, event | category | flops | bytes accessed | tf_op | source)
XLA Modules:
  0.0 98.3 jit_solution(6430046211981236982)
XLA Ops:
  0.6 95.8 %sweep.1 = (f32[32,2048]{1,0:T(8,128)}, f32[32,2048]{1,0:T(8,128)}) custom-call(s32[1,2]{1,0:T(1,128)} %modes_ref.1, bf16[1024,2048]{1,0:T(8,128)(2,1)} %bitcast.2, bf16[1024,2048]{1,0:T(8,128)(2,1)} %bitcast.3), custom_call_target="tpu_custom_call" | custom-call | tf_op jit(solution)/shard_map/sweep/pallas_call | solution.py:539
  96.4 1.8 %hand_on.1 = (f32[32,2048]{1,0:T(8,128)}, f32[32,2048]{1,0:T(8,128)}) custom-call(f32[32,2048]{1,0:T(8,128)} %get-tuple-element.4.one_in, f32[32,2048]{1,0:T(8,128)} %get-tuple-element.5.two_in), custom_call_target="tpu_custom_call" | custom-call | tf_op jit(solution)/shard_map/hand_on/pallas_call | solution.py:559
